TPU v7x, 32 devices: a whole 2x2x4 slice. The times are simulated.
32 devices in a mesh: lat: 8 (over y, x, core), lon: 4 (over z).
Axes of the slice: x: 2, y: 2, z: 4, core: 2. Of those that a mesh axis runs over, the one named last changes fastest.
Arguments:
- vorticity: float32 [2, 1280, 2560], P(None, 'lat', 'lon'), may hold values from -46 to 46
- divergence: float32 [2, 1280, 2560], P(None, 'lat', 'lon'), may hold values from -46 to 46
- height: float32 [2, 1280, 2560], P(None, 'lat', 'lon'), may hold values from -46 to 46
- mean_geopot: float32 [2], replicated, may hold values from 0.5 to 8
Outputs:
- new_vorticity: float32 [2, 1280, 2560], P(None, 'lat', 'lon')
- new_divergence: float32 [2, 1280, 2560], P(None, 'lat', 'lon')
- new_height: float32 [2, 1280, 2560], P(None, 'lat', 'lon')
All inputs are finite; a program needn't handle non-finite values.
Results may differ from a plain program's by a relative error of at most 0.0017.
Values sent between devices are 32-bit elements; how exact they have to be, the bound alone decides.
A program may use at most 448 MiB of HBM per device.

v0:
```python
import jax
import jax.numpy as jnp
from jax import lax
from jax.sharding import PartitionSpec as P

NLON = 2560
NLAT = 1280
MMAX = 1280


cap_sine = 0.5
filter_width = 64.0
diffusion = 4.0
renorm_big = 2.0**64
renorm_step = 64.0


def latitudes(row_index):
    colatitude = (4.0 * row_index + 3.0) * jnp.pi / (4.0 * NLAT + 2.0)
    shortfall = 1.0 / (8.0 * NLAT * NLAT) - 1.0 / (8.0 * NLAT * NLAT * NLAT)
    one_minus = shortfall + 2.0 * (1.0 - shortfall) * jnp.sin(0.5 * colatitude) ** 2
    one_plus = shortfall + 2.0 * (1.0 - shortfall) * jnp.cos(0.5 * colatitude) ** 2
    return (0.5 * (one_plus - one_minus), jnp.sqrt(one_minus * one_plus))


def sector_logs():
    sector_order = jnp.arange(1, MMAX, dtype=jnp.float32)
    log_terms = jnp.log2((2.0 * sector_order + 1.0) / (2.0 * sector_order))
    return jnp.concatenate([jnp.zeros((1,), jnp.float32), jnp.cumsum(log_terms)])


def fourier_table():
    points = jnp.arange(NLON, dtype=jnp.int32)
    wave_range = jnp.arange(MMAX, dtype=jnp.int32)
    phase_index = points[:, None] * wave_range[None, :] % NLON
    phase_angle = phase_index.astype(jnp.float32) * (2.0 * jnp.pi / NLON)
    return jnp.stack([jnp.cos(phase_angle), -jnp.sin(phase_angle)], axis=-1).reshape(NLON, 2 * MMAX)


def advance(recurrence, excess_degree, wave_col, cosine, wave_limit):
    previous, current, exponent = recurrence
    degree = wave_col + excess_degree
    first_row = excess_degree == 0
    growth = jnp.sqrt(
        (4.0 * degree * degree - 1.0)
        / jnp.maximum(excess_degree * (2.0 * wave_col + excess_degree), 1.0)
    )
    backward = jnp.sqrt(
        jnp.maximum((excess_degree - 1.0) * (2.0 * wave_col + excess_degree - 1.0), 0.0)
        / jnp.maximum(4.0 * (degree - 1.0) ** 2 - 1.0, 1.0)
    )
    following = growth * (cosine * current - backward * previous)
    too_large = jnp.abs(following) > renorm_big
    factor = jnp.where(too_large, 1.0 / renorm_big, 1.0)
    rescaled = (
        current * factor,
        following * factor,
        exponent + jnp.where(too_large, renorm_step, 0.0),
    )
    new_state = jax.tree.map(
        lambda kept, changed: jnp.where(first_row, kept, changed), recurrence, rescaled
    )
    row_value = new_state[1] * jnp.exp2(new_state[2])
    row_value = jnp.where(excess_degree < wave_limit, row_value, 0.0)
    return (new_state, row_value)


def legendre_blocks(wavenumbers, cumlog_part, cosine, sine_theta):
    wave_col = wavenumbers[:, None]
    log_start = -0.5 + 0.5 * cumlog_part[:, None] + wave_col * jnp.log2(sine_theta)[None, :]
    exponent = jnp.floor(log_start)
    leading = jnp.exp2(log_start - exponent)
    recurrence = (jnp.zeros_like(leading), leading, exponent)
    wave_limit = MMAX - wave_col
    cosine_row = cosine[None, :]
    legendre = jnp.zeros((wavenumbers.shape[0], MMAX, cosine.shape[0]), jnp.float32)
    anchor = jnp.zeros((), jnp.int32)

    def block_step(carry, block_index):
        state_now, table_now = carry
        row_list = []
        for offset in range(64):
            excess_degree = (block_index * 64 + offset).astype(jnp.float32)
            state_now, row_value = advance(
                state_now, excess_degree, wave_col, cosine_row, wave_limit
            )
            row_list.append(row_value)
        table_now = lax.dynamic_update_slice(
            table_now, jnp.stack(row_list, axis=1), (anchor, block_index * 64, anchor)
        )
        return ((state_now, table_now), None)

    (final_state, legendre), _ = lax.scan(
        block_step, (recurrence, legendre), jnp.arange(MMAX // 64, dtype=jnp.int32)
    )
    return legendre


def implicit(vort_part, div_part, height_part, degree, geopot):
    lap_ratio = degree * (degree + 1.0) / (MMAX * MMAX)
    coupling = jnp.sqrt(lap_ratio)
    damping = 1.0 / (1.0 + diffusion * lap_ratio * lap_ratio)
    div_new = (div_part + coupling * height_part) / (1.0 + geopot * coupling * coupling)
    height_new = height_part - geopot * coupling * div_new
    return (damping * vort_part, damping * div_new, damping * height_new)


def shards(vorticity, divergence, height, mean_geopot):
    n_lat = lax.axis_size("lat")
    n_lon = lax.axis_size("lon")
    lat_index = lax.axis_index("lat")
    lon_index = lax.axis_index("lon")
    levels = vorticity.shape[0]
    band_rows = vorticity.shape[1]
    sub_rows = band_rows // n_lon
    sectors = (
        lax.all_to_all(vorticity, "lon", split_axis=1, concat_axis=2, tiled=True),
        lax.all_to_all(divergence, "lon", split_axis=1, concat_axis=2, tiled=True),
        lax.all_to_all(height, "lon", split_axis=1, concat_axis=2, tiled=True),
    )
    stacked = jnp.stack(sectors)
    fourier = fourier_table()
    spectrum = (
        lax.dot_general(
            fourier,
            stacked,
            (((0,), (3,)), ((), ())),
            precision=lax.Precision.HIGHEST,
            preferred_element_type=jnp.float32,
        )
        / NLON
    )
    spectrum = spectrum.reshape(2 * MMAX, 3 * levels, sub_rows)
    waves_dev = MMAX // (n_lat * n_lon)
    columns = lax.all_to_all(spectrum, ("lat", "lon"), split_axis=0, concat_axis=2, tiled=True)
    row_index = jnp.arange(NLAT, dtype=jnp.int32)
    cosine, sine_theta = latitudes(row_index.astype(jnp.float32))
    weight = jnp.pi * sine_theta / (NLAT + 0.5)
    first_wave = (lat_index * n_lon + lon_index) * waves_dev
    wave_index = first_wave + jnp.arange(waves_dev, dtype=jnp.int32)
    wavenumbers = wave_index.astype(jnp.float32)
    excess = (
        jnp.maximum(wavenumbers[:, None] - MMAX * sine_theta[None, :] / cap_sine, 0.0)
        / filter_width
    )
    columns = (
        columns.reshape(waves_dev, 6 * levels, NLAT)
        * (weight[None, :] * jnp.exp(-0.5 * excess * excess))[:, None, :]
    )
    cumlog_part = lax.dynamic_slice_in_dim(sector_logs(), first_wave, waves_dev)
    legendre = legendre_blocks(wavenumbers, cumlog_part, cosine, sine_theta)
    spectral = lax.dot_general(
        columns,
        legendre,
        (((2,), (2,)), ((0,), (0,))),
        precision=lax.Precision.HIGHEST,
        preferred_element_type=jnp.float32,
    )
    spectral = spectral.reshape(waves_dev, 2, 3, levels, MMAX)
    degree = (wavenumbers[:, None] + jnp.arange(MMAX, dtype=jnp.float32)[None, :])[:, None, None, :]
    geopot = mean_geopot[None, None, :, None]
    new_v, new_d, new_h = implicit(
        spectral[:, :, 0], spectral[:, :, 1], spectral[:, :, 2], degree, geopot
    )
    updated = jnp.stack([new_v, new_d, new_h], axis=2).reshape(waves_dev, 6 * levels, MMAX)
    synthesis = lax.dot_general(
        updated,
        legendre,
        (((2,), (1,)), ((0,), (0,))),
        precision=lax.Precision.HIGHEST,
        preferred_element_type=jnp.float32,
    )
    doubling = jnp.where(wave_index == 0, 1.0, 2.0)
    synthesis = (synthesis * doubling[:, None, None]).reshape(2 * waves_dev, 3 * levels, NLAT)
    gathered = lax.all_to_all(synthesis, ("lat", "lon"), split_axis=2, concat_axis=0, tiled=True)
    result = lax.dot_general(
        gathered,
        fourier,
        (((0,), (1,)), ((), ())),
        precision=lax.Precision.HIGHEST,
        preferred_element_type=jnp.float32,
    )
    result = result.reshape(3, levels, sub_rows, NLON)
    pieces = (
        lax.all_to_all(result[0], "lon", split_axis=2, concat_axis=1, tiled=True),
        lax.all_to_all(result[1], "lon", split_axis=2, concat_axis=1, tiled=True),
        lax.all_to_all(result[2], "lon", split_axis=2, concat_axis=1, tiled=True),
    )
    return (pieces[0], pieces[1], pieces[2])


def solution(mesh):
    placed = (P(None, "lat", "lon"), P(None, "lat", "lon"), P(None, "lat", "lon"), P())
    return jax.shard_map(
        shards,
        mesh=mesh,
        in_specs=placed,
        out_specs=(P(None, "lat", "lon"), P(None, "lat", "lon"), P(None, "lat", "lon")),
        check_vma=False,
    )
```

profile of v0, /device:TPU:0, one launch (start us, length us, event | category | flops | bytes accessed | tf_op | source)
XLA Modules:
  0.0 2510.5 jit_solution(15009603203635605282)
XLA Ops:
  3.3 6.3 all-to-all-start.2
  12.7 54.7 %sine_negate_fusion = (f32[2560,1280,1]{1,0,2:T(8,128)}, f32[2560,1280,1]{1,0,2:T(8,128)}) fusion(), kind=kLoop, calls=%fused_computation.1360 | loop fusion | flops 32768000 | bytes 26214400 | tf_op jit(solution)/shard_map/neg | solution.py:37
  67.4 5.1 all-to-all-start.1
  72.5 17.5 pad_maximum_fusion
  90.1 38.9 %copy.94 = f32[2560,1280,2]{0,2,1:T(2,128)} copy(f32[2560,1280,2]{1,0,2:T(8,128)} %pad_maximum_fusion) | data formatting | bytes 52428800 | tf_op jit(solution)/shard_map/stack | solution.py:37
  129.0 31.6 %reshape.4587 = f32[2560,2560]{0,1:T(8,128)} reshape(f32[2560,1280,2]{0,2,1:T(2,128)} %copy.94) | data formatting | bytes 52428800 | tf_op jit(solution)/shard_map/reshape | solution.py:37
  162.1 5.4 all-to-all-start
  173.2 14.1 all-to-all-done
  190.0 27.4 %fusion.656 = f32[2560,3,2,40]{0,3,2,1:T(8,128)} fusion(f32[2560,2560]{0,1:T(8,128)} %reshape.4587, f32[1,2,40,2560]{3,2,1,0:T(8,128)} %stack.481, f32[1,2,40,2560]{3,2,1,0:T(8,128)S(1)} %stack.480, f32[1,2,40,2560]{3,2,1,0:T(8,128)} %stack.479), kind=kOutput, calls=%fused_computation.1366 | convolution fusion | flops 18876211200 | bytes 31129600 | tf_op jit(solution)/shard_map/dot_general | solution.py:124
  217.3 7.1 copy.102
  224.4 10.2 reshape.4919
  234.6 3.8 all-to-all-start.3
  238.4 79.4 %broadcast_in_dim.1016.clone = f32[40,1280,1280]{2,1,0:T(8,128)} broadcast(f32[]{:T(128)} %constant.863.clone.1), dimensions={} | broadcast | bytes 262144000 | tf_op jit(solution)/shard_map/broadcast_in_dim | solution.py:76
  317.9 1575.2 %while.23 = (s32[]{:T(128)}, f32[40,1280]{1,0:T(8,128)S(1)}, f32[40,1280]{1,0:T(8,128)S(1)}, f32[40,1280]{1,0:T(8,128)S(1)}, f32[40,1280,1280]{2,1,0:T(8,128)}, ...) while((s32[]{:T(128)}, f32[40,1280]{1,0:T(8,128)S(1)}, ...), condition=%wide.region_3.4_spmd.clone.clone.clone.clone, body=%wide.region_2.3_spmd.clone.clone.clone.clone.sunk | while | flops 78823744 | bytes 129213056 | solution.py:93
  398.3 13.7 copy_dynamic-update-slice_fusion.2
  476.1 13.8 copy_dynamic-update-slice_fusion.2
  554.1 13.7 copy_dynamic-update-slice_fusion.2
  631.9 13.8 copy_dynamic-update-slice_fusion.2
  709.9 13.8 copy_dynamic-update-slice_fusion.2
  787.9 13.9 copy_dynamic-update-slice_fusion.2
  865.9 13.8 copy_dynamic-update-slice_fusion.2
  943.8 13.7 copy_dynamic-update-slice_fusion.2
  1021.7 13.8 copy_dynamic-update-slice_fusion.2
  1099.7 13.7 copy_dynamic-update-slice_fusion.2
  1177.6 13.8 copy_dynamic-update-slice_fusion.2
  1255.5 13.8 copy_dynamic-update-slice_fusion.2
  1333.5 13.8 copy_dynamic-update-slice_fusion.2
  1411.5 13.7 copy_dynamic-update-slice_fusion.2
  1489.3 13.7 copy_dynamic-update-slice_fusion.2
  1567.2 13.9 copy_dynamic-update-slice_fusion.2
  1645.2 13.8 copy_dynamic-update-slice_fusion.2
  1723.2 13.8 copy_dynamic-update-slice_fusion.2
  1801.2 13.7 copy_dynamic-update-slice_fusion.2
  1879.1 13.6 copy_dynamic-update-slice_fusion.2
  1894.7 8.2 reduce.4
  1902.9 7.5 reshape.4920
  1910.4 11.7 copy.104
  1922.1 7.6 reshape.4589
  1929.7 219.3 %fusion.660 = f32[40,12,1280]{2,1,0:T(8,128)} fusion(f32[40,1280,1280]{2,1,0:T(8,128)} %get-tuple-element.647, f32[40,12,1280]{2,1,0:T(8,128)S(1)} %reshape.4589, f32[40,1280]{1,0:T(8,128)S(1)} %copy-done.1), kind=kOutput, calls=%fused_computation.1369 | convolution fusion | flops 9437798400 | bytes 267264000 | tf_op jit(solution)/shard_map/dot_general | solution.py:152
  2149.0 3.4 copy.106
  2154.1 132.1 %convolution_multiply_fusion = f32[40,12,1280]{2,1,0:T(8,128)} fusion(f32[40,1280,1280]{2,1,0:T(8,128)} %get-tuple-element.647, f32[40,12,1280]{2,0,1:T(8,128)S(1)} %bitcast.2377, f32[40]{0:T(128)S(1)} %compare_select_fusion), kind=kOutput, calls=%fused_computation.1367 | convolution fusion | flops 9437798400 | bytes 267059360 | tf_op jit(solution)/shard_map/dot_general | solution.py:166
  2286.2 2.8 reshape.4594
  2289.0 3.7 copy.109
  2292.6 7.6 reshape.4921
  2300.2 62.1 %all_to_all.132 = f32[32,1,19200]{2,1,0:T(1,128)S(1)} all-to-all(f32[32,1,19200]{2,1,0:T(1,128)} %reshape.4921), channel_id=1, replica_groups=mesh['lat'=8,'lon'=4] {'lat','lon'}, dimensions={0} | all-to-all | bytes 4915200 | tf_op jit(solution)/shard_map/all_to_all | solution.py:175
  2362.3 8.6 reduce.5
  2370.9 6.5 reshape.4922
  2377.3 6.7 copy.111
  2384.1 4.3 all_to_all.111
  2388.4 24.4 fusion.646
  2415.4 5.6 reshape.4923
  2421.0 4.0 all-to-all-start.5
  2427.7 5.6 reshape.4925
  2433.3 13.6 all-to-all-done.5
  2446.9 4.2 all-to-all-start.6
  2453.9 5.6 reshape.4927
  2459.5 12.8 all-to-all-done.6
  2472.3 4.5 all-to-all-start.7
  2476.7 3.9 reduce.6
  2480.7 5.7 reshape.4924
  2488.5 4.0 reduce.7
  2492.4 4.5 reshape.4926
  2499.4 4.0 reduce.8
  2503.4 4.5 reshape.4928
  (3309 shorter events, 1297.6 us)
Async XLA Ops:
  3.3 64.1 %all-to-all-start.2 = ((f32[2,160,640]{2,0,1:T(2,128)}), f32[2,160,640]{2,0,1:T(2,128)S(1)}, u32[]{:S(2)}, u32[]{:S(2)}) async-start(f32[2,160,640]{2,0,1:T(2,128)} %copy.99), calls=%async_computation.2 | async-start | bytes 1638400 | tf_op jit(solution)/shard_map/all_to_all | solution.py:119
  67.4 94.7 %all-to-all-start.1 = ((f32[2,160,640]{2,0,1:T(2,128)}), f32[2,160,640]{2,0,1:T(2,128)S(1)}, u32[]{:S(2)}, u32[]{:S(2)}) async-start(f32[2,160,640]{2,0,1:T(2,128)} %copy.97), calls=%async_computation.1 | async-start | bytes 1638400 | tf_op jit(solution)/shard_map/all_to_all | solution.py:118
  129.0 31.6 %copy-start.3 = (f32[2,160,640]{2,1,0:T(8,128)S(1)}, f32[2,160,640]{2,1,0:T(8,128)}, u32[]{:S(2)}) copy-start(f32[2,160,640]{2,1,0:T(8,128)} %param.6) | copy-start | bytes 2457604
  162.1 25.1 %all-to-all-start = ((f32[2,160,640]{2,0,1:T(2,128)}), f32[2,160,640]{2,0,1:T(2,128)}, u32[]{:S(2)}, u32[]{:S(2)}) async-start(f32[2,160,640]{2,0,1:T(2,128)} %copy.95), calls=%async_computation | async-start | bytes 1638400 | tf_op jit(solution)/shard_map/all_to_all | solution.py:117
  234.6 1659.5 %all-to-all-start.3 = ((f32[32,1,19200]{2,1,0:T(1,128)}), f32[32,1,19200]{2,1,0:T(1,128)}, u32[]{:S(2)}, u32[]{:S(2)}) async-start(f32[32,1,19200]{2,1,0:T(1,128)} %reshape.4919), calls=%async_computation.3 | async-start | bytes 4915200 | tf_op jit(solution)/shard_map/all_to_all | solution.py:135
  238.4 79.5 %copy-start = (f32[40,1280]{1,0:T(8,128)S(1)}, f32[40,1280]{1,0:T(8,128)}, u32[]{:S(2)}) copy-start(f32[40,1280]{1,0:T(8,128)} %custom-call) | copy-start | bytes 614404
  317.9 1575.2 %copy-start.2 = (f32[40,1280]{1,0:T(8,128)S(1)}, f32[40,1280]{1,0:T(8,128)}, u32[]{:S(2)}) copy-start(f32[40,1280]{1,0:T(8,128)} %get-tuple-element.1282) | copy-start | bytes 614404
  317.9 1575.2 %copy-start.4 = (f32[2]{0:T(128)S(1)}, f32[2]{0:T(128)}, u32[]{:S(2)}) copy-start(f32[2]{0:T(128)} %param.9) | copy-start | bytes 28
  1910.4 19.3 copy-start.1
  2421.0 25.9 %all-to-all-start.5 = ((f32[4,1,51200]{2,1,0:T(1,128)}), f32[4,1,51200]{2,1,0:T(1,128)S(1)}, u32[]{:S(2)}, u32[]{:S(2)}) async-start(f32[4,1,51200]{2,1,0:T(1,128)} %reshape.4923), calls=%async_computation.5 | async-start | bytes 1638400 | tf_op jit(solution)/shard_map/all_to_all | solution.py:185
  2446.9 25.4 %all-to-all-start.6 = ((f32[4,1,51200]{2,1,0:T(1,128)}), f32[4,1,51200]{2,1,0:T(1,128)}, u32[]{:S(2)}, u32[]{:S(2)}) async-start(f32[4,1,51200]{2,1,0:T(1,128)} %reshape.4925), calls=%async_computation.6 | async-start | bytes 1638400 | tf_op jit(solution)/shard_map/all_to_all | solution.py:186
  2472.3 27.1 %all-to-all-start.7 = ((f32[4,1,51200]{2,1,0:T(1,128)}), f32[4,1,51200]{2,1,0:T(1,128)}, u32[]{:S(2)}, u32[]{:S(2)}) async-start(f32[4,1,51200]{2,1,0:T(1,128)} %reshape.4927), calls=%async_computation.7 | async-start | bytes 1638400 | tf_op jit(solution)/shard_map/all_to_all | solution.py:187
where the time goes:
time: 2520 us; the launch traced here: 2510 us
  other arithmetic  1360 us (54%)
  local copies, waits for them, and re-layouts  576 us (23%)
  matrix products  403 us (16%)
  blocking collectives  62.1 us (2%)
  waiting for transfers between devices  40.5 us (2%)
  loops' own time  36.4 us (1%)
  starting transfers between devices  33.2 us (1%)
    while x1260, other arithmetic  1200 us
    dynamic_update_slice x20, local copies, waits for them, and re-layouts, block_step(): lax.dynamic_update_slice(table_now, jnp.stack(row_list, axis=1), (anchor,...  275 us
    dot_general x1, matrix products, shards(): lax.dot_general(columns, legendre, (((2,), (2,)), ((0,), (0,))), precisio...  219 us
    dot_general x1, matrix products, shards(): lax.dot_general(updated, legendre, (((2,), (1,)), ((0,), (0,))), precisio...  132 us
    broadcast_in_dim x1, local copies, waits for them, and re-layouts, legendre_blocks(): jnp.zeros((wavenumbers.shape[0], MMAX, cosine.shape[0]), jnp.float32)  79.4 us
    unnamed x23, local copies, waits for them, and re-layouts  70 us
    all_to_all x1, blocking collectives, shards(): lax.all_to_all(synthesis, ('lat', 'lon'), split_axis=2, concat_axis=0, ti...  62.1 us
    neg x1, other arithmetic, fourier_table(): -jnp.sin(phase_angle)  54.7 us
  transfers between devices with their start and end apart: 7, of which 3 were waited for; matrix products, arithmetic and copies ran while one was open for 72% of the time, Pallas kernels for 0%

commit v1 on v0

v1 whole, which is shorter than its diff:
```python
import functools

import jax
import jax.numpy as jnp
import ml_dtypes
import numpy as np
from jax import lax
from jax.experimental import pallas as pl
from jax.experimental.pallas import tpu as pltpu
from jax.sharding import PartitionSpec as P

NLON = 2560
NLAT = 1280
MMAX = 1280
HALF = NLAT // 2

cap_sine = 0.5
filter_width = 64.0
diffusion = 4.0

PACK = 8
GROUP = 8
STEPS = 32
ROWS = GROUP * STEPS
LANES = 256
USED = 192
CHECK = 8
BIG = 2.0**16
DOWN = 2.0**-64


def plan(n_dev):
    waves_dev = MMAX // n_dev
    if waves_dev % GROUP == 0:
        blocks = np.arange(MMAX).reshape(waves_dev // GROUP, n_dev, GROUP)
        blocks[1::2] = blocks[1::2, ::-1].copy()
        return np.transpose(blocks, (1, 0, 2)).reshape(n_dev, waves_dev)
    return np.arange(MMAX).reshape(n_dev, waves_dev)


def first_waves(n_dev, device, group):
    waves_dev = MMAX // n_dev
    if waves_dev % GROUP == 0:
        forth = group * n_dev + device
        back = (group + 1) * n_dev - 1 - device
        return GROUP * jnp.where(group % 2 == 0, forth, back)
    return device * waves_dev + GROUP * group


def fourier_table(n_dev):
    waves = plan(n_dev)
    waves_dev = waves.shape[1]
    groups = -(-waves_dev // GROUP)
    phase = (np.arange(NLON)[:, None] * waves.reshape(-1)[None, :]) % NLON
    angle = 2.0 * np.pi / NLON * np.arange(NLON)
    parts = np.stack([np.cos(angle)[phase], -np.sin(angle)[phase]], axis=1)
    parts = parts.reshape(NLON, 2, n_dev, waves_dev)
    parts = np.pad(parts, ((0, 0), (0, 0), (0, 0), (0, groups * GROUP - waves_dev)))
    parts = parts.reshape(NLON, 2, n_dev, groups, GROUP).transpose(0, 2, 3, 1, 4)
    parts = parts.reshape(NLON, n_dev * groups * 16)
    top = parts.astype(ml_dtypes.bfloat16)
    rest = (parts - top.astype(np.float64)).astype(ml_dtypes.bfloat16)
    return top, rest


def latitudes(row_index):
    colatitude = (4.0 * row_index + 3.0) * jnp.pi / (4.0 * NLAT + 2.0)
    shortfall = 1.0 / (8.0 * NLAT * NLAT) - 1.0 / (8.0 * NLAT * NLAT * NLAT)
    one_minus = shortfall + 2.0 * (1.0 - shortfall) * jnp.sin(0.5 * colatitude) ** 2
    one_plus = shortfall + 2.0 * (1.0 - shortfall) * jnp.cos(0.5 * colatitude) ** 2
    return (0.5 * (one_plus - one_minus), jnp.sqrt(one_minus * one_plus))


def sector_logs():
    sector_order = jnp.arange(1, MMAX, dtype=jnp.float32)
    log_terms = jnp.log2((2.0 * sector_order + 1.0) / (2.0 * sector_order))
    return jnp.concatenate([jnp.zeros((1,), jnp.float32), jnp.cumsum(log_terms)])


def split(value):
    top = value.astype(jnp.bfloat16)
    rest = (value - top.astype(jnp.float32)).astype(jnp.bfloat16)
    return top, rest


def split_outside(value):
    rounded = lax.reduce_precision(value, exponent_bits=8, mantissa_bits=7)
    return rounded.astype(jnp.bfloat16), (value - rounded).astype(jnp.bfloat16)


def matmul(left, right):
    return lax.dot_general(
        left, right, (((1,), (0,)), ((), ())), preferred_element_type=jnp.float32
    )


def legendre_kernel(
    n_dev, levels, geopot_ref, cosine_ref, lead_ref, expo_ref, coef_ref, filter_ref, in_ref,
    out_ref, table_a, table_b, field_top, field_rest, total, prev_ref, cur_ref, exp_ref, turned,
    ready,
):
    device = lax.axis_index("lat") * lax.axis_size("lon") + lax.axis_index("lon")
    first = first_waves(n_dev, device, pl.program_id(0))
    pairs = lax.div(MMAX - first + 2 * STEPS - 1, 2 * STEPS)

    sub_rows = NLAT // n_dev
    packs = n_dev // PACK
    lane = lax.broadcasted_iota(jnp.int32, (sub_rows, 128), 1)
    sign = jnp.where((lane // 32) % 2 == 0, 1.0, -1.0)

    def at(row_block):
        return pl.ds(row_block * sub_rows, sub_rows)

    for pack in range(packs):
        block = in_ref[pack * PACK : (pack + 1) * PACK, 0].reshape(PACK * 16, LANES)
        turned[pack] = jnp.transpose(block, (1, 0))
    for north in range(n_dev // 2):
        south = n_dev - 1 - north
        weight = filter_ref[0, at(north), :]

        def gather(source, which, place):
            rows = pl.ds(which * sub_rows, sub_rows)
            value = turned[source // PACK, rows, :]
            return pltpu.roll(value, (place - (source % PACK) * 16) % 128, 1)

        halves = [jnp.zeros((sub_rows, 128), jnp.float32)] * 2
        for which in range(3 * levels):
            kind, level = which // levels, which % levels
            for parity in range(2):
                place = (kind % 2) * 64 + parity * 32 + level * 16
                value = gather(north, which, place) + sign * gather(south, which, place)
                here = (lane >= place) & (lane < place + 16)
                halves[kind // 2] = jnp.where(here, value, halves[kind // 2])
        for half in range(2):
            top, rest = split(halves[half] * weight)
            field_top[at(north), half * 128 : (half + 1) * 128] = top
            field_top[pl.ds(HALF + north * sub_rows, sub_rows), half * 128 : (half + 1) * 128] = top
            field_rest[at(north), half * 128 : (half + 1) * 128] = rest
    total[...] = jnp.zeros_like(total)

    lane = lax.broadcasted_iota(jnp.int32, (GROUP, 128), 1)
    sub = lax.broadcasted_iota(jnp.int32, (GROUP, 128), 0)
    same = lane % GROUP == sub
    even = jnp.where(same & ((lane // 32) % 2 == 0), 1.0, 0.0)
    odd = jnp.where(same & ((lane // 32) % 2 == 1), 1.0, 0.0)
    second_level = (lane // 16) % 2 == 1
    geopot = jnp.where(second_level, geopot_ref[1], geopot_ref[0])
    is_div = lane < 64
    cosine = jnp.broadcast_to(cosine_ref[...], (GROUP, HALF))

    def generate(chunk, table_ref):
        coefs = coef_ref[0, chunk]
        previous, current, exponent = prev_ref[...], cur_ref[...], exp_ref[...]
        values = []
        for step in range(STEPS):
            if step % CHECK == 0:
                large = jnp.abs(current) > BIG
                factor = jnp.where(large, DOWN, 1.0)
                current = current * factor
                previous = previous * factor
                exponent = exponent + jnp.where(large, 1.0, 0.0)
                scale = jnp.where(exponent >= 0.0, 1.0, jnp.where(exponent >= -1.0, DOWN, 0.0))
            forward = coefs[:, step : step + 1]
            backward = coefs[:, STEPS + step : STEPS + step + 1]
            previous, current = current, forward * (cosine * current) - backward * previous
            values.append(current * scale)
            if len(values) == 2:
                top, rest = split(jnp.concatenate(values, axis=0))
                place = pl.ds((step - 1) * GROUP, 2 * GROUP)
                table_ref[place, :HALF] = top
                table_ref[place, HALF:] = rest
                values = []
        prev_ref[...], cur_ref[...], exp_ref[...] = previous, current, exponent

    def transform(chunk, table_ref):
        spectral = matmul(table_ref[...], field_top[...])
        spectral += matmul(table_ref[:, :HALF], field_rest[...])
        coefs = coef_ref[0, chunk]

        def coef(which, step):
            place = which * STEPS + step
            return jnp.broadcast_to(coefs[:, place : place + 1], (GROUP, 128))

        left, right = [], []
        for step in range(STEPS):
            rows = slice(step * GROUP, (step + 1) * GROUP)
            first_half, height = spectral[rows, :128], spectral[rows, 128:]
            coupling = coef(2, step)
            damping = coef(3, step) * (even if step % 2 == 0 else odd)
            inverse = jnp.where(second_level, coef(5, step), coef(4, step))
            div_new = (first_half + coupling * height) * inverse
            height_new = height - geopot * coupling * div_new
            left.append(jnp.where(is_div, div_new, first_half) * damping)
            right.append(height_new * damping)
        updated = jnp.concatenate(
            [jnp.concatenate(left, axis=0), jnp.concatenate(right, axis=0)], axis=1
        )
        flipped = jnp.transpose(updated, (1, 0))[:USED]
        new_top, new_rest = split(flipped)
        both = matmul(jnp.concatenate([new_top, new_rest], axis=0), table_ref[:, :HALF])
        total[...] += both[:USED] + both[USED:] + matmul(new_top, table_ref[:, HALF:])

    prev_ref[...] = lead_ref[0]
    cur_ref[...] = jnp.zeros_like(cur_ref)
    exp_ref[...] = expo_ref[0]
    generate(0, table_a)

    def body(pair, carry):
        generate(2 * pair + 1, table_b)
        transform(2 * pair, table_a)
        generate(2 * pair + 2, table_a)
        transform(2 * pair + 1, table_b)
        return carry

    lax.fori_loop(0, pairs, body, 0)

    summed = jnp.transpose(total[...], (1, 0))
    ready[:, :USED] = summed
    lane = lax.broadcasted_iota(jnp.int32, (sub_rows, 128), 1)
    for pack in range(packs):
        for which in range(3 * levels):
            kind, level = which // levels, which % levels
            value = jnp.zeros((sub_rows, 128), jnp.float32)
            for slot in range(PACK):
                target = pack * PACK + slot
                north = target < n_dev // 2
                rows = at(target if north else n_dev - 1 - target)
                source = ready[rows, (kind // 2) * 128 : (kind // 2 + 1) * 128]
                place = (kind % 2) * 64 + level * 16
                even_part = pltpu.roll(source, (slot * 16 - place) % 128, 1)
                odd_part = pltpu.roll(source, (slot * 16 - place - 32) % 128, 1)
                joined = even_part + odd_part if north else even_part - odd_part
                here = (lane >= slot * 16) & (lane < slot * 16 + 16)
                value = jnp.where(here, joined, value)
            turned[pack, pl.ds(which * sub_rows, sub_rows), :] = value
        out_ref[pack * PACK : (pack + 1) * PACK, 0] = jnp.transpose(turned[pack], (1, 0)).reshape(
            PACK, 16, LANES
        )


def legendre_step(n_dev, levels, mean_geopot, cosine, lead, expo, coefs, filtering, columns):
    groups = columns.shape[1]
    chunks = coefs.shape[1]
    return pl.pallas_call(
        functools.partial(legendre_kernel, n_dev, levels),
        grid=(groups,),
        out_shape=jax.ShapeDtypeStruct(columns.shape, jnp.float32),
        in_specs=[
            pl.BlockSpec(memory_space=pltpu.SMEM),
            pl.BlockSpec((1, HALF), lambda i: (0, 0)),
            pl.BlockSpec((1, GROUP, HALF), lambda i: (i, 0, 0)),
            pl.BlockSpec((1, GROUP, HALF), lambda i: (i, 0, 0)),
            pl.BlockSpec((1, chunks, GROUP, 6 * STEPS), lambda i: (i, 0, 0, 0)),
            pl.BlockSpec((1, HALF, 128), lambda i: (i, 0, 0)),
            pl.BlockSpec((n_dev, 1, 16, LANES), lambda i: (0, i, 0, 0)),
        ],
        out_specs=pl.BlockSpec((n_dev, 1, 16, LANES), lambda i: (0, i, 0, 0)),
        scratch_shapes=[pltpu.VMEM((ROWS, 2 * HALF), jnp.bfloat16)] * 2
        + [pltpu.VMEM((2 * HALF, LANES), jnp.bfloat16), pltpu.VMEM((HALF, LANES), jnp.bfloat16)]
        + [pltpu.VMEM((USED, HALF), jnp.float32)]
        + [pltpu.VMEM((GROUP, HALF), jnp.float32)] * 3
        + [pltpu.VMEM((n_dev // PACK, LANES, PACK * 16), jnp.float32)]
        + [pltpu.VMEM((HALF, LANES), jnp.float32)],
        compiler_params=pltpu.CompilerParams(vmem_limit_bytes=40 * 2**20),
    )(mean_geopot, cosine[None, :], lead, expo, coefs, filtering, columns)


def coefficients(waves, mean_geopot):
    groups = waves.shape[0]
    chunks = MMAX // STEPS + 2
    wave = waves[:, None, :, None]
    excess = jnp.arange(chunks * STEPS, dtype=jnp.float32).reshape(1, chunks, 1, STEPS)
    degree = wave + excess
    growth = jnp.sqrt(
        (4.0 * degree * degree - 1.0) / jnp.maximum(excess * (2.0 * wave + excess), 1.0)
    )
    backward = jnp.sqrt(
        jnp.maximum((excess - 1.0) * (2.0 * wave + excess - 1.0), 0.0)
        / jnp.maximum(4.0 * (degree - 1.0) ** 2 - 1.0, 1.0)
    )
    start = excess == 0.0
    lap_ratio = degree * (degree + 1.0) / (MMAX * MMAX)
    damping = jnp.where(degree < MMAX, 1.0 / (1.0 + diffusion * lap_ratio * lap_ratio), 0.0)
    damping = damping * jnp.where(wave == 0.0, 1.0, 2.0)
    kinds = [
        jnp.where(start, 0.0, growth),
        jnp.where(start, -1.0, growth * backward),
        jnp.sqrt(lap_ratio),
        damping,
        1.0 / (1.0 + mean_geopot[0] * lap_ratio),
        1.0 / (1.0 + mean_geopot[1] * lap_ratio),
    ]
    shape = (groups, chunks, GROUP, STEPS)
    return jnp.concatenate([jnp.broadcast_to(kind, shape) for kind in kinds], axis=-1)


def shards(vorticity, divergence, height, mean_geopot):
    n_lat = lax.axis_size("lat")
    n_lon = lax.axis_size("lon")
    n_dev = n_lat * n_lon
    device = lax.axis_index("lat") * n_lon + lax.axis_index("lon")
    levels = vorticity.shape[0]
    sub_rows = vorticity.shape[1] // n_lon
    waves_dev = MMAX // n_dev
    groups = -(-waves_dev // GROUP)

    kinds = 3 * levels
    rows = kinds * sub_rows
    southern = lax.axis_index("lat") >= n_lat // 2

    def mirror(value):
        return jnp.where(southern, jnp.flip(value, 1), value)

    def exchange(value, axes):
        return lax.all_to_all(value, axes, split_axis=0, concat_axis=0, tiled=True)

    stacked = jnp.stack([divergence, vorticity, height])
    stacked = stacked.reshape(kinds, n_lon, sub_rows, NLON // n_lon)
    sectors = exchange(jnp.moveaxis(stacked, 1, 0), "lon")
    sectors = mirror(jnp.transpose(sectors, (1, 2, 0, 3)).reshape(kinds, sub_rows, NLON))
    sectors = jnp.pad(sectors.reshape(rows, NLON), ((0, LANES - rows), (0, 0)))
    table_top, table_rest = (jnp.asarray(part) for part in fourier_table(n_dev))
    top, rest = split_outside(sectors)
    across = functools.partial(
        lax.dot_general,
        dimension_numbers=(((0,), (1,)), ((), ())),
        preferred_element_type=jnp.float32,
    )
    spectrum = across(table_top, top) + across(table_top, rest) + across(table_rest, top)
    columns = exchange(spectrum.reshape(n_dev, groups, 16, LANES), ("lat", "lon"))

    first = first_waves(n_dev, device, jnp.arange(groups))
    waves = (first[:, None] + jnp.arange(GROUP)[None, :]).astype(jnp.float32)
    cosine, sine_theta = latitudes(jnp.arange(HALF, dtype=jnp.float32))
    weight = jnp.pi * sine_theta / (NLAT + 0.5) / NLON
    lane_waves = jnp.tile(waves, (1, 16))[:, None, :]
    excess = (
        jnp.maximum(lane_waves - MMAX * sine_theta[:, None] / cap_sine, 0.0) / filter_width
    )
    filtering = weight[:, None] * jnp.exp(-0.5 * excess * excess)

    cumlog = jnp.take(sector_logs(), jnp.minimum(waves.astype(jnp.int32), MMAX - 1))
    log_start = -0.5 + 0.5 * cumlog[:, :, None] + waves[:, :, None] * jnp.log2(sine_theta)
    exponent = jnp.floor(log_start)
    leading = jnp.exp2(log_start - exponent)
    turns = jnp.floor((exponent + 48.0) / 64.0)
    lead = leading * jnp.exp2(exponent - 64.0 * turns)

    synthesis = legendre_step(
        n_dev, levels, mean_geopot, cosine, lead, turns, coefficients(waves, mean_geopot),
        filtering, columns,
    )
    gathered = exchange(synthesis, ("lat", "lon")).reshape(-1, LANES)
    top, rest = split_outside(gathered)
    back = functools.partial(
        lax.dot_general,
        dimension_numbers=(((0,), (1,)), ((), ())),
        preferred_element_type=jnp.float32,
    )
    result = back(top, table_top) + back(rest, table_top) + back(top, table_rest)
    result = mirror(result[:rows].reshape(kinds, sub_rows, NLON))
    result = result.reshape(kinds, sub_rows, n_lon, NLON // n_lon)
    pieces = exchange(jnp.transpose(result, (2, 0, 1, 3)), "lon")
    pieces = jnp.moveaxis(pieces, 0, 1).reshape(3, levels, n_lon * sub_rows, NLON // n_lon)
    return (pieces[1], pieces[0], pieces[2])


def solution(mesh):
    placed = P(None, "lat", "lon")
    return jax.shard_map(
        shards,
        mesh=mesh,
        in_specs=(placed, placed, placed, P()),
        out_specs=(placed, placed, placed),
        check_vma=False,
    )
```

time: 2520 us -> 465 us (0.18)
  other arithmetic: 1360 us -> 10.9 us
  local copies, waits for them, and re-layouts: 576 us -> 36.7 us
  matrix products: 403 us -> 37.4 us
  Pallas kernels: 0 us -> 143 us
  waiting for transfers between devices: 40.5 us -> 101 us
  blocking collectives: 62.1 us -> 122 us
  loops' own time: 36.4 us -> 0 us
    while x1260 -> x0, other arithmetic: 1200 us -> none
    dot_general x4 -> x6, matrix products: 403 us -> 37.4 us  [the longest x1 6.9 us: shards(): across(table_top, top) + across(table_top, rest) + across(table_rest, top)]
    dynamic_update_slice x20 -> x0, local copies, waits for them, and re-layouts: 275 us -> none  [block_step(): lax.dynamic_update_slice(table_now, jnp.stack(row_list, axis=1), (anchor,...]
    pallas_call x0 -> x1, Pallas kernels: none -> 143 us  [legendre_step(): pl.pallas_call(functools.partial(legendre_kernel, n_dev, levels), grid=(g...]
    broadcast_in_dim x1 -> x0, local copies, waits for them, and re-layouts: 79.4 us -> none  [legendre_blocks(): jnp.zeros((wavenumbers.shape[0], MMAX, cosine.shape[0]), jnp.float32)]
    unnamed x23 -> x16, local copies, waits for them, and re-layouts: 70 us -> 5.65 us
    all_to_all x1 -> x2, blocking collectives: 62.1 us -> 122 us  [exchange(): return lax.all_to_all(value, axes, split_axis=0, concat_axis=0, tiled=True)]
    all_to_all x7 -> x2, waiting for transfers between devices: 40.5 us -> 101 us  [exchange(): return lax.all_to_all(value, axes, split_axis=0, concat_axis=0, tiled=True)]
  transfers between devices with their start and end apart: 7 -> 2, of which waited for: 3 -> 2; matrix products, arithmetic and copies ran while one was open for 72% -> 3% of each run, Pallas kernels for 0% -> 0%
where the time goes in v1:
time: 465 us; the launch traced here: 464 us
  Pallas kernels  143 us (31%)
  blocking collectives  122 us (26%)
  waiting for transfers between devices  101 us (22%)
  matrix products  37.4 us (8%)
  local copies, waits for them, and re-layouts  36.7 us (8%)
  starting transfers between devices  11.2 us (2%)
  other arithmetic  10.9 us (2%)
    pallas_call x1, Pallas kernels, legendre_step(): pl.pallas_call(functools.partial(legendre_kernel, n_dev, levels), grid=(g...  143 us
    all_to_all x2, blocking collectives, exchange(): return lax.all_to_all(value, axes, split_axis=0, concat_axis=0, tiled=True)  122 us
    all_to_all x2, waiting for transfers between devices, exchange(): return lax.all_to_all(value, axes, split_axis=0, concat_axis=0, tiled=True)  101 us
    rev x2, local copies, waits for them, and re-layouts, mirror(): return jnp.where(southern, jnp.flip(value, 1), value)  14.2 us
    all_to_all x2, starting transfers between devices, exchange(): return lax.all_to_all(value, axes, split_axis=0, concat_axis=0, tiled=True)  11.2 us
  transfers between devices with their start and end apart: 2, of which 2 were waited for; matrix products, arithmetic and copies ran while one was open for 3% of the time, Pallas kernels for 0%

profile of v1, /device:TPU:0, one launch (start us, length us, event | category | flops | bytes accessed | tf_op | source)
XLA Modules:
  0.0 464.4 jit_solution(13008727859508010231)
XLA Ops:
  0.6 1.8 pad_maximum_fusion
  2.4 1.6 copy.16
  4.1 6.3 %all-to-all-start = ((f32[4,6,40,640]{3,2,1,0:T(8,128)}), f32[4,6,40,640]{3,2,1,0:T(8,128)S(1)}, u32[]{:S(2)}, u32[]{:S(2)}) async-start(f32[4,6,40,640]{3,2,1,0:T(8,128)} %copy.16), calls=%async_computation | async-start | bytes 4915200 | tf_op jit(solution)/shard_map/all_to_all | solution.py:315
  10.4 55.9 %all-to-all-done = f32[4,6,40,640]{3,2,1,0:T(8,128)S(1)} async-done(((f32[4,6,40,640]{3,2,1,0:T(8,128)}), f32[4,6,40,640]{3,2,1,0:T(8,128)S(1)}, u32[]{:S(2)}, u32[]{:S(2)}) %all-to-all-start) | async-done | bytes 2457632 | tf_op jit(solution)/shard_map/all_to_all | solution.py:315
  66.3 0.0 copy-start.3
  66.3 1.5 copy-done.3
  67.8 2.0 copy.21
  69.8 7.1 %rev.7 = f32[6,40,2560]{2,1,0:T(8,128)} reverse(f32[6,40,2560]{2,1,0:T(8,128)S(1)} %bitcast.44), dimensions={1} | reverse | bytes 4915200 | tf_op jit(solution)/shard_map/jit(_flip)/rev | solution.py:312
  76.9 0.0 slice-start
  76.9 0.3 broadcast_select_fusion.1
  77.1 0.0 slice-start.1
  77.1 0.0 slice-start.2
  77.2 0.0 slice-start.3
  77.2 6.9 %fusion.33 = f32[256,2560]{1,0:T(8,128)S(1)} fusion(bf16[2560,2560]{1,0:T(8,128)(2,1)} %constant.150.clone, f32[240,2560]{1,0:T(8,128)S(1)} %bitcast.51), kind=kOutput, calls=%fused_computation.54 | convolution fusion | flops 3356753920 | bytes 18186240 | tf_op jit(solution)/shard_map/dot_general | solution.py:329
  84.1 0.0 slice-done
  84.1 0.1 slice-done.1
  84.1 1.2 slice-done.2
  85.3 0.0 slice-done.3
  85.4 3.5 convolution_add_fusion.1
  88.9 6.8 %fusion = f32[2560,256]{0,1:T(8,128)S(1)} fusion(f32[256,2560]{1,0:T(8,128)S(1)} %convolution_add_fusion.1, bf16[2560,2560]{1,0:T(8,128)(2,1)} %constant.151.clone, f32[240,2560]{1,0:T(8,128)S(1)} %bitcast.53), kind=kOutput, calls=%fused_computation.2 | convolution fusion | flops 3357409280 | bytes 20807680 | tf_op jit(solution)/shard_map/dot_general | solution.py:329
  95.7 2.1 copy.18
  97.8 4.9 %all-to-all-start.1 = ((f32[32,5,16,256]{3,2,1,0:T(8,128)}), f32[32,5,16,256]{3,2,1,0:T(8,128)S(1)}, u32[]{:S(2)}, u32[]{:S(2)}) async-start(f32[32,5,16,256]{3,2,1,0:T(8,128)} %bitcast.46), calls=%async_computation.1 | async-start | bytes 5242880 | tf_op jit(solution)/shard_map/all_to_all | solution.py:315
  102.7 0.0 copy-start.2
  102.7 0.1 compare_select_fusion
  102.8 0.1 reshape.411
  102.9 0.3 reduce-window.9
  103.2 0.1 slice.42
  103.3 0.1 slice_reduce_fusion
  103.4 0.1 add_bitcast_fusion
  103.5 0.1 pad_maximum_fusion.1
  103.6 0.8 gather_fusion
  104.4 0.1 reshape.410
  104.4 0.0 copy-done.2
  104.4 0.6 fusion.56
  106.3 0.1 add_convert_fusion
  106.4 0.1 tile.9
  106.5 0.1 fusion.50
  106.6 3.3 fusion.31
  109.9 4.7 %concatenate.7.coef_ref = f32[5,42,8,192]{3,2,1,0:T(8,128)} concatenate(f32[5,42,8,32]{3,2,1,0:T(8,128)} %get-tuple-element.13, f32[5,42,8,32]{3,2,1,0:T(8,128)} %get-tuple-element.14, f32[5,42,8,32]{3,2,1,0:T(8,128)} %get-tuple-element.15, f32[5,42,8,32]{3,2,1,0:T(8,128)} %get-tuple-element.11, f32[5,42,8,32]{3,2,1,0:T(8,128)} %get-tuple-element.12, ...), dimensions={3} | concatenate | bytes 2580480 | tf_op jit(solution)/shard_map/concatenate | solution.py:294
  114.6 0.1 subtract_multiply_fusion.cosine_ref
  114.7 0.1 log_multiply_fusion
  114.8 0.1 sqrt_multiply_fusion
  114.8 0.1 fusion.38
  115.0 1.7 exponential_multiply_fusion.filter_ref
  116.7 44.8 %all-to-all-done.1.in_ref = f32[32,5,16,256]{3,2,1,0:T(8,128)S(1)} async-done(((f32[32,5,16,256]{3,2,1,0:T(8,128)}), f32[32,5,16,256]{3,2,1,0:T(8,128)S(1)}, u32[]{:S(2)}, u32[]{:S(2)}) %all-to-all-start.1) | async-done | bytes 2621472 | tf_op jit(solution)/shard_map/all_to_all | solution.py:315
  161.5 0.0 copy-start
  161.5 1.5 copy-done
  162.9 0.0 copy-start.1
  162.9 1.4 copy-done.1
  164.4 142.9 %shard_map.85 = f32[32,5,16,256]{3,2,1,0:T(8,128)S(1)} custom-call(f32[2]{0:T(128)S(1)} %copy-done.2, f32[1,640]{1,0:T(1,128)S(1)} %subtract_multiply_fusion.cosine_ref, f32[5,8,640]{2,1,0:T(8,128)S(1)} %get-tuple-element.17.lead_ref, f32[5,8,640]{2,1,0:T(8,128)S(1)} %get-tuple-element.16.expo_ref, f32[5,42,8,192]{3,2,1,0:T(8,128)S(1)} %copy-done, ...), custom_call_target="tpu_custom_call" | custom-call | tf_op jit(solution)/shard_map/pallas_call | solution.py:244
  307.3 62.5 %all_to_all.20 = f32[32,5,16,256]{3,2,1,0:T(8,128)S(1)} all-to-all(f32[32,5,16,256]{3,2,1,0:T(8,128)S(1)} %shard_map.85), channel_id=1, replica_groups=mesh['lat'=8,'lon'=4] {'lat','lon'}, dimensions={0} | all-to-all | bytes 5242880 | tf_op jit(solution)/shard_map/all_to_all | solution.py:315
  369.7 0.4 fusion.2
  370.1 6.7 %fusion.57 = f32[256,2560]{1,0:T(8,128)S(1)} fusion(bf16[2560,256]{1,0:T(8,128)(2,1)S(1)} %get-tuple-element.4, bf16[2560,2560]{1,0:T(8,128)(2,1)} %constant.150.clone), kind=kOutput, calls=%fused_computation.100 | convolution fusion | flops 3355443200 | bytes 17039360 | tf_op jit(solution)/shard_map/dot_general | solution.py:360
  376.9 6.7 %fusion.59 = f32[256,2560]{1,0:T(8,128)S(1)} fusion(bf16[2560,256]{1,0:T(8,128)(2,1)S(1)} %get-tuple-element.4, bf16[2560,2560]{1,0:T(8,128)(2,1)} %constant.151.clone), kind=kOutput, calls=%fused_computation.102 | convolution fusion | flops 3355443200 | bytes 17039360 | tf_op jit(solution)/shard_map/dot_general | solution.py:360
  383.6 6.7 %fusion.58 = f32[256,2560]{1,0:T(8,128)S(1)} fusion(bf16[2560,256]{1,0:T(8,128)(2,1)S(1)} %get-tuple-element.3, bf16[2560,2560]{1,0:T(8,128)(2,1)} %constant.150.clone), kind=kOutput, calls=%fused_computation.101 | convolution fusion | flops 3355443200 | bytes 17039360 | tf_op jit(solution)/shard_map/dot_general | solution.py:360
  390.3 0.6 slice_add_fusion
  390.9 7.1 %rev.8 = f32[6,40,2560]{2,1,0:T(8,128)} reverse(f32[6,40,2560]{2,1,0:T(8,128)S(1)} %bitcast.42), dimensions={1} | reverse | bytes 4915200 | tf_op jit(solution)/shard_map/jit(_flip)/rev | solution.py:312
  398.0 1.7 broadcast_select_fusion
  399.8 2.7 reshape.408
  402.5 0.2 copy.19
  402.7 60.0 %all_to_all.21 = f32[4,6,40,640]{3,2,1,0:T(8,128)S(1)} all-to-all(f32[4,6,40,640]{3,2,1,0:T(8,128)S(1)} %copy.19), channel_id=1, replica_groups=mesh['lat'=8,'lon'=4] {'lon'}, dimensions={0} | all-to-all | bytes 4915200 | tf_op jit(solution)/shard_map/all_to_all | solution.py:315
  462.7 0.2 copy.23
  462.9 1.5 fusion.55
  (9 shorter events, 0.1 us)
Async XLA Ops:
  4.1 62.2 %all-to-all-start = ((f32[4,6,40,640]{3,2,1,0:T(8,128)}), f32[4,6,40,640]{3,2,1,0:T(8,128)S(1)}, u32[]{:S(2)}, u32[]{:S(2)}) async-start(f32[4,6,40,640]{3,2,1,0:T(8,128)} %copy.16), calls=%async_computation | async-start | bytes 4915200 | tf_op jit(solution)/shard_map/all_to_all | solution.py:315
  66.3 1.5 copy-start.3
  76.9 7.2 %slice-start = ((s8[13107200]{0:T(1024)(128)(4,1)}), s8[4194304]{0:T(1024)(128)(4,1)S(1)}, s32[]{:S(2)}) async-start(s8[13107200]{0:T(1024)(128)(4,1)} %bitcast.61), calls=%async_computation.4 | async-start | bytes 8388608
  77.1 7.0 %slice-start.1 = ((s8[13107200]{0:T(1024)(128)(4,1)}), s8[4194304]{0:T(1024)(128)(4,1)S(1)}, s32[]{:S(2)}) async-start(s8[13107200]{0:T(1024)(128)(4,1)} %bitcast.61), calls=%async_computation.5 | async-start | bytes 8388608
  77.1 8.2 %slice-start.2 = ((s8[13107200]{0:T(1024)(128)(4,1)}), s8[4194304]{0:T(1024)(128)(4,1)S(1)}, s32[]{:S(2)}) async-start(s8[13107200]{0:T(1024)(128)(4,1)} %bitcast.61), calls=%async_computation.6 | async-start | bytes 8388608
  77.2 8.2 %slice-start.3 = ((s8[13107200]{0:T(1024)(128)(4,1)}), s8[524288]{0:T(1024)(128)(4,1)S(1)}, s32[]{:S(2)}) async-start(s8[13107200]{0:T(1024)(128)(4,1)} %bitcast.61), calls=%async_computation.7 | async-start | bytes 1048576
  97.8 63.7 %all-to-all-start.1 = ((f32[32,5,16,256]{3,2,1,0:T(8,128)}), f32[32,5,16,256]{3,2,1,0:T(8,128)S(1)}, u32[]{:S(2)}, u32[]{:S(2)}) async-start(f32[32,5,16,256]{3,2,1,0:T(8,128)} %bitcast.46), calls=%async_computation.1 | async-start | bytes 5242880 | tf_op jit(solution)/shard_map/all_to_all | solution.py:315
  102.7 1.7 copy-start.2
  161.5 1.5 copy-start
  162.9 1.4 copy-start.1
